TPU v7x, 32 devices: a whole 2x2x4 slice. The times are simulated.
32 devices in a mesh: seq: 8 (over z, x), head: 4 (over y, core).
Axes of the slice: x: 2, y: 2, z: 4, core: 2. Of those that a mesh axis runs over, the one named last changes fastest.
Arguments:
- tokens: bfloat16 [8192, 4096], P('seq'), may hold values from -6 to 6
- w_query: bfloat16 [4096, 4096], P(None, 'head'), may hold values from -0.09375 to 0.09375
- w_key: bfloat16 [4096, 4096], P(None, 'head'), may hold values from -0.09375 to 0.09375
- w_value: bfloat16 [4096, 4096], P(None, 'head'), may hold values from -0.09375 to 0.09375
- norm_gain: float32 [4096], P('head'), may hold values from 0.25 to 1.75
- w_out: bfloat16 [4096, 4096], P('head'), may hold values from -0.125 to 0.125
Outputs:
- mixed: bfloat16 [8192, 4096], P('seq', 'head')
All inputs are finite; a program needn't handle non-finite values.
Results may differ from a plain program's by a relative error of at most 0.02.
Values may be sent and summed in bfloat16 or wider, within the bound.
A program may use at most 128 MiB of HBM per device.

v0:
```python
import jax
import jax.numpy as jnp
from jax import lax
from jax.sharding import PartitionSpec as P

HEAD_DIM = 128
SPAN = 128


def prefix(shard, axis, combine, identity):
    size, index = (lax.axis_size(axis), lax.axis_index(axis))
    everything = lax.all_gather(shard.astype(jnp.bfloat16), axis)
    start = jnp.broadcast_to(jnp.asarray(identity, shard.dtype), shard.shape)

    def hop(k, before):
        reached = k < index
        new = combine(before, everything[k].astype(shard.dtype))
        return jnp.where(reached, new, before)

    return lax.fori_loop(0, size, hop, start)


def lower_mask(size):
    rows = lax.broadcasted_iota(jnp.int32, (size, size), 0)
    cols = lax.broadcasted_iota(jnp.int32, (size, size), 1)
    return (rows >= cols).astype(jnp.float32)


def add_states(earlier, later):
    return earlier + later


def local(tokens, w_query, w_key, w_value, norm_gain, w_out):
    count = tokens.shape[0]
    width = w_query.shape[1]
    heads_here = width // HEAD_DIM
    blocks = count // SPAN
    shape4 = (blocks, SPAN, heads_here, HEAD_DIM)
    q_rows = (
        jnp.dot(tokens, w_query, preferred_element_type=jnp.float32)
        .astype(jnp.bfloat16)
        .reshape(shape4)
    )
    k_rows = (
        jnp.dot(tokens, w_key, preferred_element_type=jnp.float32)
        .astype(jnp.bfloat16)
        .reshape(shape4)
    )
    v_rows = (
        jnp.dot(tokens, w_value, preferred_element_type=jnp.float32)
        .astype(jnp.bfloat16)
        .reshape(shape4)
    )
    scores = jnp.einsum("cihd,cjhd->chij", q_rows, k_rows, preferred_element_type=jnp.float32)
    scores = (scores * lower_mask(SPAN)).astype(jnp.bfloat16)
    within = jnp.einsum("chij,cjhe->cihe", scores, v_rows, preferred_element_type=jnp.float32)
    states = jnp.einsum("cjhd,cjhe->chde", k_rows, v_rows, preferred_element_type=jnp.float32)
    running = jnp.cumsum(states, axis=0)
    earlier = jnp.concatenate([jnp.zeros_like(states[:1]), running[:-1]], axis=0)
    total = running[-1]
    empty = jnp.zeros_like(total)
    carried = prefix(total, "seq", add_states, empty)
    applied = (carried[None] + earlier).astype(jnp.bfloat16)
    across = jnp.einsum("cihd,chde->cihe", q_rows, applied, preferred_element_type=jnp.float32)
    raw_out = within + across
    power = jnp.mean(raw_out * raw_out, axis=-1, keepdims=True)
    normed = raw_out * lax.rsqrt(power + 1e-06) * norm_gain.reshape(heads_here, HEAD_DIM)
    attended = normed.astype(jnp.bfloat16).reshape(count, width)
    summed = lax.psum_scatter(
        lax.dot_general(
            w_out, attended, (((0,), (1,)), ((), ())), preferred_element_type=jnp.float32
        ).astype(jnp.bfloat16),
        "head",
        scatter_dimension=0,
        tiled=True,
    ).astype(jnp.float32)
    return summed.T.astype(jnp.bfloat16)


def solution(mesh):
    in_specs = (
        P("seq", None),
        P(None, "head"),
        P(None, "head"),
        P(None, "head"),
        P("head"),
        P("head", None),
    )
    out_specs = P("seq", "head")
    return jax.shard_map(local, mesh=mesh, in_specs=in_specs, out_specs=out_specs, check_vma=False)
```

profile of v0, /device:TPU:26, one launch (start us, length us, event | category | flops | bytes accessed | tf_op | source)
XLA Modules:
  0.0 210.2 jit_solution(13746249327276649673)
XLA Ops:
  6.5 13.7 %convert_bitcast_fusion.1 = bf16[128,8,8,128]{3,1,2,0:T(8,128)(2,1)S(1)} fusion(bf16[1024,4096]{1,0:T(8,128)(2,1)} %param.8, bf16[4096,1024]{1,0:T(8,128)(2,1)} %param.10), kind=kOutput, calls=%fused_computation.13 | convolution fusion | flops 8590983168 | bytes 18874368 | tf_op jit(solution)/shard_map/dot_general | solution.py:45
  20.2 1.9 copy.29
  22.2 3.3 %copy.21 = bf16[8,128,8,128]{1,3,2,0:T(8,128)(2,1)S(1)} copy(bf16[8,128,8,128]{3,2,1,0:T(8,128)(2,1)} %bitcast.49) | data formatting | bytes 4194304 | tf_op jit(solution)/shard_map/reshape | solution.py:47
  25.4 14.4 %convert_bitcast_fusion.3 = bf16[128,8,8,128]{3,1,2,0:T(8,128)(2,1)S(1)} fusion(bf16[1024,4096]{1,0:T(8,128)(2,1)} %param.8, bf16[4096,1024]{1,0:T(8,128)(2,1)} %param.11), kind=kOutput, calls=%fused_computation.15 | convolution fusion | flops 8590983168 | bytes 18874368 | tf_op jit(solution)/shard_map/dot_general | solution.py:50
  39.9 0.6 copy.27
  40.5 1.3 copy-done.1
  41.8 0.7 fusion.8
  42.5 3.9 %fusion.16 = f32[8,8,128,128]{3,2,1,0:T(8,128)S(1)} fusion(f32[8,8,128,128]{3,2,1,0:T(8,128)S(1)} %fusion.8), kind=kOutput, calls=%fused_computation.27 | output fusion | flops 7340032 | bytes 8388608 | tf_op jit(solution)/shard_map/jit(cumsum)/reduce_window_sum | solution.py:58
  46.4 1.9 copy-done.2
  48.4 0.7 slice.12
  49.1 0.0 all-gather.2.cloned.1.call-update
  49.1 0.2 reduce-scatter.2.cloned.1.call-start
  49.4 4.3 %slice.10 = f32[7,8,128,128]{3,2,1,0:T(8,128)} slice(f32[8,8,128,128]{3,2,1,0:T(8,128)} %copy-done.2), slice={[0:7], [0:8], [0:128], [0:128]} | slice | bytes 7340032 | tf_op jit(solution)/shard_map/slice | solution.py:59
  53.7 13.7 %convert_bitcast_fusion.2 = bf16[128,8,8,128]{3,1,2,0:T(8,128)(2,1)S(1)} fusion(bf16[1024,4096]{1,0:T(8,128)(2,1)} %param.8, bf16[4096,1024]{1,0:T(8,128)(2,1)} %param.9), kind=kOutput, calls=%fused_computation.14 | convolution fusion | flops 8590983168 | bytes 18874368 | tf_op jit(solution)/shard_map/dot_general | solution.py:40
  67.4 0.6 copy.28
  68.1 6.3 %fusion.6 = f32[8,8,128,128]{3,2,1,0:T(8,128)} fusion(bf16[8,128,8,128]{3,2,1,0:T(8,128)(2,1)} %bitcast.48, bf16[8,128,8,128]{1,3,2,0:T(8,128)(2,1)} %copy-done, f32[128,128]{1,0:T(8,128)S(1)} %fusion.14, bf16[8,128,8,128]{3,2,1,0:T(8,128)(2,1)S(1)} %bitcast.45), kind=kOutput, calls=%fused_computation.16 | convolution fusion | flops 538968064 | bytes 10551296 | tf_op jit(solution)/shard_map/chij,cjhe->cihe/dot_general | solution.py:56
  74.4 22.7 %all-gather.2.cloned.1.call-done = bf16[8,8,128,128]{3,2,1,0:T(8,128)(2,1)} async-done(((bf16[1,8,128,128]{3,2,1,0:T(8,128)(2,1)}), bf16[8,8,128,128]{3,2,1,0:T(8,128)(2,1)}) %all-gather.2.cloned.1.call-update) | async-done | bytes 2097168 | tf_op jit(solution)/shard_map/all_gather | solution.py:12
  97.1 10.0 %while.14 = (s32[]{:T(128)}, f32[8,128,128]{2,1,0:T(8,128)S(1)}, s32[]{:T(128)}, bf16[8,8,128,128]{3,2,1,0:T(8,128)(2,1)}, s32[]{:T(128)}, /*index=5*/s32[]{:T(128)}) while((s32[]{:T(128)}, f32[8,128,128]{2,1,0:T(8,128)S(1)}, s32[]{:T(128)}, bf16[8,8,128,128]{3,2,1,0:T(8,128)(2,1)}, s32[]{:T(128)}, /*index=5*/s32[]{:T(128)}) %tuple.33), condition=%wide.region_2.3_spmd.clone, body=%wide.region_1.2_spmd.clone.sunk | while | flops 524292 | bytes 1310813 | solution.py:20
  97.1 1.2 add_select_fusion.2
  98.4 1.2 add_select_fusion.2
  99.6 1.2 add_select_fusion.2
  100.9 1.2 add_select_fusion.2
  102.1 1.2 add_select_fusion.2
  103.4 1.2 add_select_fusion.2
  104.6 1.2 add_select_fusion.2
  105.9 1.2 add_select_fusion.2
  107.2 4.9 %fusion = (f32[8,128,8]{1,2,0:T(8,128)S(1)}, f32[8,8,128,128]{3,2,1,0:T(8,128)S(1)}) fusion(f32[8,8,128,128]{3,2,1,0:T(8,128)} %fusion.6, bf16[8,128,8,128]{3,2,1,0:T(8,128)(2,1)S(1)} %bitcast.46, f32[7,8,128,128]{3,2,1,0:T(8,128)} %slice.10, f32[8,128,128]{2,1,0:T(8,128)S(1)} %get-tuple-element.84), kind=kOutput, calls=%fused_computation.4 | convolution fusion | flops 273670144 | bytes 14712832 | tf_op jit(solution)/shard_map/cihd,chde->cihe/dot_general | solution.py:64
  112.1 0.8 fusion.2
  113.0 2.8 %copy.25 = bf16[8,128,8,128]{3,2,1,0:T(8,128)(2,1)} copy(bf16[8,128,8,128]{1,3,2,0:T(8,128)(2,1)S(1)} %fusion.2) | data formatting | bytes 4194304 | tf_op jit(solution)/shard_map/convert_element_type | solution.py:68
  115.8 14.7 %convert_bitcast_fusion = bf16[4096,1024]{0,1:T(8,128)(2,1)} fusion(bf16[1024,4096]{1,0:T(8,128)(2,1)} %param.13, bf16[128,8,8,128]{3,2,1,0:T(8,128)(2,1)} %bitcast.50), kind=kOutput, calls=%fused_computation.1 | convolution fusion | flops 8594128896 | bytes 18874368 | tf_op jit(solution)/shard_map/dot_general | solution.py:70
  130.5 0.0 reduce-scatter.2.cloned.1.call-update
  130.5 72.8 %reduce-scatter.2.cloned.1.call-done = bf16[1024,1024]{0,1:T(8,128)(2,1)} async-done(((bf16[4096,1024]{0,1:T(8,128)(2,1)}), bf16[1024,1024]{0,1:T(8,128)(2,1)}) %reduce-scatter.2.cloned.1.call-update) | async-done | bytes 2097168 | tf_op jit(solution)/shard_map/reduce_scatter | solution.py:69
  (10 shorter events, 0.0 us)
Async XLA Ops:
  6.5 90.6 %all-gather.2.cloned.1.call-start = ((), (), s32[]{:S(2)}) async-start(), calls=%async_computation.1 | async-start | bytes 2359296 | tf_op jit(solution)/shard_map/all_gather | solution.py:12
  25.4 15.1 %copy-start = (bf16[8,128,8,128]{1,3,2,0:T(8,128)(2,1)}, bf16[8,128,8,128]{1,3,2,0:T(8,128)(2,1)S(1)}, u32[]{:S(2)}) copy-start(bf16[8,128,8,128]{1,3,2,0:T(8,128)(2,1)S(1)} %copy.21) | copy-start | bytes 6291460
  40.5 1.3 copy-start.1
  46.4 1.9 copy-start.2
  49.1 154.2 %reduce-scatter.2.cloned.1.call-start = ((), (), s32[]{:S(2)}) async-start(), calls=%async_computation.2 | async-start | bytes 10485760 | tf_op jit(solution)/shard_map/reduce_scatter | solution.py:69
  107.2 5.0 %copy-start.3 = (f32[1024]{0:T(1024)S(1)}, f32[1024]{0:T(1024)}, u32[]{:S(2)}) copy-start(f32[1024]{0:T(1024)} %param.12) | copy-start | bytes 12292
Sparse Core Ops, SparseCore 0:
  49.3 47.7 all-gather.1
  130.6 72.6 reduce-scatter.1
where the time goes:
time: 212 us; the launch traced here: 210 us
  waiting for transfers between devices  95.6 us (45%)
  matrix products  68.5 us (32%)
  local copies, waits for them, and re-layouts  17.5 us (8%)
  other arithmetic  14.6 us (7%)
  between operations  13.5 us (6%)
    reduce_scatter x1, waiting for transfers between devices, local(): lax.psum_scatter(lax.dot_general(w_out, attended, (((0,), (1,)), ((), ())...  72.8 us
    all_gather x1, waiting for transfers between devices, prefix(): everything = lax.all_gather(shard.astype(jnp.bfloat16), axis)  22.7 us
    dot_general x1, matrix products, local(): lax.dot_general(w_out, attended, (((0,), (1,)), ((), ())), preferred_elem...  14.7 us
    dot_general x1, matrix products, local(): jnp.dot(tokens, w_value, preferred_element_type=jnp.float32)  14.4 us
    dot_general x1, matrix products, local(): jnp.dot(tokens, w_query, preferred_element_type=jnp.float32)  13.7 us
    dot_general x1, matrix products, local(): jnp.dot(tokens, w_key, preferred_element_type=jnp.float32)  13.7 us
    select_n x8, other arithmetic, hop(): return jnp.where(reached, new, before)  9.87 us
    unnamed x11, local copies, waits for them, and re-layouts  6.44 us
  transfers between devices with their start and end apart: 2, of which 2 were waited for; matrix products, arithmetic and copies ran while one was open for 12% of the time, Pallas kernels for 0%

commit v1 on v0

v1 whole, which is shorter than its diff:
```python
import functools

import jax
import jax.numpy as jnp
from jax import lax
from jax.experimental import pallas as pl
from jax.experimental.pallas import tpu as pltpu
from jax.sharding import PartitionSpec as P

HEAD_DIM = 128
CHUNK = 256
PAIR = 2 * HEAD_DIM
ROWS = 512
AHEAD = 2
MESH = pl.DeviceIdType.MESH
BF16 = jnp.bfloat16
F32 = jnp.float32


def kernel(
    n_seq, n_head,
    tok_hbm, wq_hbm, wk_hbm, wv_hbm, gain_ref, wo_hbm, out_hbm,
    tok, kbuf, vbuf, wq, wo, q, k, v, att, pre, total, carried,
    scan_out, scan_in, sib_out, sib_in, y_out, y_in, own, obuf,
    tok_sem, k_sem, v_sem, wq_sem, wo_sem, o_sem,
    scan_ss, scan_rs, sib_ss, sib_rs, y_ss, y_rs,
):
    count, depth = tok.shape
    width = q.shape[1]
    heads = width // HEAD_DIM
    pairs = width // PAIR
    cols = wo.shape[1] // n_head
    nt = count // CHUNK
    ny = n_head // 2
    rounds = (n_seq - 1).bit_length()
    s = lax.axis_index("seq")
    h = lax.axis_index("head")
    y, c = h // 2, h % 2
    sib = y * 2 + 1 - c

    def tok_copy(t):
        rows = pl.ds(pl.multiple_of(t * CHUNK, CHUNK), CHUNK)
        return pltpu.make_async_copy(tok_hbm.at[rows], tok.at[rows], tok_sem.at[t])

    def panel(src, dst, sem, p):
        return pltpu.make_async_copy(
            src.at[:, pl.ds(p * PAIR, PAIR)], dst.at[p % 2], sem.at[p % 2]
        )

    wq_copy = pltpu.make_async_copy(wq_hbm, wq, wq_sem)
    wo_copy = pltpu.make_async_copy(wo_hbm, wo, wo_sem)

    panel(wk_hbm, kbuf, k_sem, 0).start()
    for t in range(nt):
        tok_copy(t).start()
    panel(wv_hbm, vbuf, v_sem, 0).start()

    barrier = pltpu.get_barrier_semaphore()
    expected = jnp.int32(ny)
    pl.semaphore_signal(barrier, inc=1, device_id=(s, sib), device_id_type=MESH)
    for j in range(1, ny):
        peer = lax.rem(y + j, ny) * 2 + c
        pl.semaphore_signal(barrier, inc=1, device_id=(s, peer), device_id_type=MESH)
    for r in range(rounds):
        d = 1 << r

        @pl.when(s + d < n_seq)
        def _():
            pl.semaphore_signal(barrier, inc=1, device_id=(s + d, h), device_id_type=MESH)

        @pl.when(s >= d)
        def _():
            pl.semaphore_signal(barrier, inc=1, device_id=(s - d, h), device_id_type=MESH)

        expected += (s + d < n_seq).astype(jnp.int32) + (s >= d).astype(jnp.int32)
    pl.semaphore_wait(barrier, expected)

    def scan_copy(p, r):
        return pltpu.make_async_remote_copy(
            src_ref=scan_out.at[p, r], dst_ref=scan_in.at[p, r],
            send_sem=scan_ss.at[p, r], recv_sem=scan_rs.at[p, r],
            device_id=(lax.rem(s + (1 << r), n_seq), h), device_id_type=MESH,
        )

    def scan_send(p, r):
        @pl.when(s + (1 << r) < n_seq)
        def _():
            scan_out[p, r] = (carried[2 * p:2 * p + 2] + total[2 * p:2 * p + 2]).astype(BF16)
            scan_copy(p, r).start()

    def scan_recv(p, r):
        @pl.when(s >= (1 << r))
        def _():
            scan_copy(p, r).wait_recv()
            carried[2 * p:2 * p + 2] += scan_in[p, r].astype(F32)

    stage = [0] * pairs

    def scan_step(done):
        for p in range(done):
            r = stage[p]
            if r > rounds:
                continue
            if r > 0:
                scan_recv(p, r - 1)
            if r < rounds:
                scan_send(p, r)
            stage[p] = r + 1

    carried[...] = jnp.zeros_like(carried)

    def project(w, dst, p, wait):
        @pl.loop(0, count // ROWS)
        def _(i):
            if wait:
                for j in range(ROWS // CHUNK):
                    tok_copy(i * (ROWS // CHUNK) + j).wait()
            rows = pl.ds(pl.multiple_of(i * ROWS, ROWS), ROWS)
            dst[rows, p * PAIR:(p + 1) * PAIR] = jnp.dot(
                tok[rows, :], w[...], preferred_element_type=F32
            ).astype(BF16)

    for p in range(pairs):
        panel(wk_hbm, kbuf, k_sem, p).wait()
        if p + 1 < pairs:
            panel(wk_hbm, kbuf, k_sem, p + 1).start()
            panel(wv_hbm, vbuf, v_sem, p + 1).start()
        if p == min(1, pairs - 1):
            wq_copy.start()
            wo_copy.start()
        project(kbuf.at[p % 2], k, p, p == 0)
        if p > 0:
            scan_step(p)
        panel(wv_hbm, vbuf, v_sem, p).wait()
        project(vbuf.at[p % 2], v, p, False)
        for e in range(2):
            hd = 2 * p + e
            lanes = slice(hd * HEAD_DIM, (hd + 1) * HEAD_DIM)
            run = jnp.zeros((HEAD_DIM, HEAD_DIM), F32)
            for t in range(nt):
                pre[t, hd] = run
                run = run + lax.dot_general(
                    k[t * CHUNK:(t + 1) * CHUNK, lanes], v[t * CHUNK:(t + 1) * CHUNK, lanes],
                    (((0,), (0,)), ((), ())), preferred_element_type=F32,
                )
            total[hd] = run
        scan_step(p + 1)

    def project_q(t):
        rows = pl.ds(pl.multiple_of(t * CHUNK, CHUNK), CHUNK)

        @pl.loop(0, pairs)
        def _(i):
            lanes = pl.ds(pl.multiple_of(i * PAIR, PAIR), PAIR)
            q[rows, lanes] = jnp.dot(
                tok[rows, :], wq[:, lanes], preferred_element_type=F32
            ).astype(BF16)

    wq_copy.wait()
    for t in range(AHEAD):
        project_q(t)
        scan_step(pairs)
    while min(stage) <= rounds:
        scan_step(pairs)
    wo_copy.wait()

    def sib_copy(t, j):
        return pltpu.make_async_remote_copy(
            src_ref=sib_out.at[t % 2, j], dst_ref=sib_in.at[t, j],
            send_sem=sib_ss.at[t, j], recv_sem=sib_rs.at[t, j],
            device_id=(s, sib), device_id_type=MESH,
        )

    def y_copy(t, j):
        return pltpu.make_async_remote_copy(
            src_ref=y_out.at[t, j - 1], dst_ref=y_in.at[t, j - 1],
            send_sem=y_ss.at[t, j - 1], recv_sem=y_rs.at[t, j - 1],
            device_id=(s, lax.rem(y + j, ny) * 2 + c), device_id_type=MESH,
        )

    def partial(dest):
        lanes = pl.ds(pl.multiple_of(dest * cols, cols), cols)
        return jnp.dot(att[...], wo[:, lanes], preferred_element_type=F32)

    order = list(range(1, ny)) + [0]

    @pl.loop(0, nt)
    def _(t):
        rows = pl.ds(pl.multiple_of(t * CHUNK, CHUNK), CHUNK)
        keep = lax.broadcasted_iota(jnp.int32, (CHUNK, CHUNK), 0) >= lax.broadcasted_iota(
            jnp.int32, (CHUNK, CHUNK), 1
        )
        for hd in range(heads):
            lanes = slice(hd * HEAD_DIM, (hd + 1) * HEAD_DIM)
            qh, kh, vh = q[rows, lanes], k[rows, lanes], v[rows, lanes]
            scores = lax.dot_general(
                qh, kh, (((1,), (1,)), ((), ())), preferred_element_type=F32
            )
            scores = jnp.where(keep, scores, 0.0).astype(BF16)
            prior = (carried[hd] + pre[t, hd]).astype(BF16)
            raw = jnp.dot(scores, vh, preferred_element_type=F32) + jnp.dot(
                qh, prior, preferred_element_type=F32
            )
            power = jnp.mean(raw * raw, axis=-1, keepdims=True)
            att[:, lanes] = (raw * lax.rsqrt(power + 1e-6) * gain_ref[:, lanes]).astype(BF16)

        @pl.when(t >= 2)
        def _():
            for j in range(ny):
                sib_copy(t - 2, j).wait_send()

        for j in order:
            sib_out[t % 2, j] = partial(lax.rem(y + j, ny) * 2 + 1 - c).astype(BF16)
            sib_copy(t, j).start()
        own[rows, :] = partial(h)
        for j in range(1, ny):
            mine = partial(lax.rem(y + j, ny) * 2 + c)
            sib_copy(t, j).wait_recv()
            y_out[t, j - 1] = (mine + sib_in[t, j].astype(F32)).astype(BF16)
            y_copy(t, j).start()
        sib_copy(t, 0).wait_recv()
        own[rows, :] += sib_in[t, 0].astype(F32)

        @pl.when(t + AHEAD < nt)
        def _():
            project_q(t + AHEAD)

    def out_copy(t):
        rows = pl.ds(t * CHUNK, CHUNK)
        return pltpu.make_async_copy(obuf.at[t % 2], out_hbm.at[rows], o_sem.at[t % 2])

    for t in range(nt):
        if t >= 2:
            out_copy(t - 2).wait()
        result = own[t * CHUNK:(t + 1) * CHUNK, :]
        for j in range(1, ny):
            y_copy(t, j).wait_recv()
            result = result + y_in[t, j - 1].astype(F32)
        obuf[t % 2] = result.astype(BF16)
        out_copy(t).start()
    for t in range(max(nt - 2, 0), nt):
        out_copy(t).wait()
        for j in range(ny):
            sib_copy(t, j).wait_send()
    for t in range(nt):
        for j in range(1, ny):
            y_copy(t, j).wait_send()
    for p in range(pairs):
        for r in range(rounds):
            @pl.when(s + (1 << r) < n_seq)
            def _():
                scan_copy(p, r).wait_send()


def local(n_seq, n_head, tokens, w_query, w_key, w_value, norm_gain, w_out):
    count, depth = tokens.shape
    width = w_query.shape[1]
    heads, pairs = width // HEAD_DIM, width // PAIR
    features = w_out.shape[1]
    cols = features // n_head
    nt, ny = count // CHUNK, n_head // 2
    rounds = (n_seq - 1).bit_length()
    dma = pltpu.SemaphoreType.DMA
    hbm = pl.BlockSpec(memory_space=pl.ANY)
    vmem = pl.BlockSpec(memory_space=pltpu.VMEM)
    return pl.pallas_call(
        functools.partial(kernel, n_seq, n_head),
        out_shape=jax.ShapeDtypeStruct((count, cols), BF16),
        in_specs=[hbm, hbm, hbm, hbm, vmem, hbm],
        out_specs=hbm,
        scratch_shapes=[
            pltpu.VMEM((count, depth), BF16),
            pltpu.VMEM((2, depth, PAIR), BF16),
            pltpu.VMEM((2, depth, PAIR), BF16),
            pltpu.VMEM((depth, width), BF16),
            pltpu.VMEM((width, features), BF16),
            pltpu.VMEM((count, width), BF16),
            pltpu.VMEM((count, width), BF16),
            pltpu.VMEM((count, width), BF16),
            pltpu.VMEM((CHUNK, width), BF16),
            pltpu.VMEM((nt, heads, HEAD_DIM, HEAD_DIM), F32),
            pltpu.VMEM((heads, HEAD_DIM, HEAD_DIM), F32),
            pltpu.VMEM((heads, HEAD_DIM, HEAD_DIM), F32),
            pltpu.VMEM((pairs, rounds, 2, HEAD_DIM, HEAD_DIM), BF16),
            pltpu.VMEM((pairs, rounds, 2, HEAD_DIM, HEAD_DIM), BF16),
            pltpu.VMEM((2, ny, CHUNK, cols), BF16),
            pltpu.VMEM((nt, ny, CHUNK, cols), BF16),
            pltpu.VMEM((nt, ny - 1, CHUNK, cols), BF16),
            pltpu.VMEM((nt, ny - 1, CHUNK, cols), BF16),
            pltpu.VMEM((count, cols), F32),
            pltpu.VMEM((2, CHUNK, cols), BF16),
            dma((nt,)), dma((2,)), dma((2,)), dma, dma, dma((2,)),
            dma((pairs, rounds)), dma((pairs, rounds)),
            dma((nt, ny)), dma((nt, ny)),
            dma((nt, ny - 1)), dma((nt, ny - 1)),
        ],
        compiler_params=pltpu.CompilerParams(
            collective_id=0, has_side_effects=True, vmem_limit_bytes=63 * 2**20
        ),
    )(tokens, w_query, w_key, w_value, norm_gain.reshape(1, width), w_out)


def solution(mesh):
    n_seq, n_head = mesh.shape["seq"], mesh.shape["head"]
    in_specs = (
        P("seq", None), P(None, "head"), P(None, "head"), P(None, "head"),
        P("head"), P("head", None),
    )
    return jax.shard_map(
        functools.partial(local, n_seq, n_head), mesh=mesh, in_specs=in_specs,
        out_specs=P("seq", "head"), check_vma=False,
    )
```

time: 212 us -> 94.2 us (0.44)
  waiting for transfers between devices: 95.6 us -> 0 us
  Pallas kernels: 0 us -> 90.9 us
  matrix products: 68.5 us -> 0 us
  other arithmetic: 14.6 us -> 0 us
  local copies, waits for them, and re-layouts: 17.5 us -> 3.08 us
  between operations: 13.5 us -> 0.01 us
    pallas_call x0 -> x1, Pallas kernels: none -> 90.9 us  [local(): pl.pallas_call(functools.partial(kernel, n_seq, n_head), out_shape=jax.Sh...]
    reduce_scatter x1 -> x0, waiting for transfers between devices: 72.8 us -> none  [local(): lax.psum_scatter(lax.dot_general(w_out, attended, (((0,), (1,)), ((), ())...]
    dot_general x7 -> x0, matrix products: 68.5 us -> none  [the longest x1 14.7 us: local(): lax.dot_general(w_out, attended, (((0,), (1,)), ((), ())), preferred_elem...]
    all_gather x1 -> x0, waiting for transfers between devices: 22.7 us -> none  [prefix(): everything = lax.all_gather(shard.astype(jnp.bfloat16), axis)]
    select_n x8 -> x0, other arithmetic: 9.87 us -> none  [hop(): return jnp.where(reached, new, before)]
    slice x2 -> x0, local copies, waits for them, and re-layouts: 5.03 us -> none  [the longest x1 4.29 us: local(): running[:-1]]
    another operation x1 -> x0, other arithmetic: 3.89 us -> none  [local(): running = jnp.cumsum(states, axis=0)]
    unnamed x11 -> x1, local copies, waits for them, and re-layouts: 6.44 us -> 3.08 us
  transfers between devices with their start and end apart: 2 -> 0, of which waited for: 2 -> 0; matrix products, arithmetic and copies ran while one was open for 12% -> 0% of each run, Pallas kernels for 0% -> 0%
where the time goes in v1:
time: 94.2 us; the launch traced here: 94 us
  Pallas kernels  90.9 us (96%)
  local copies, waits for them, and re-layouts  3.08 us (3%)
    pallas_call x1, Pallas kernels, local(): pl.pallas_call(functools.partial(kernel, n_seq, n_head), out_shape=jax.Sh...  90.9 us
    unnamed x1, local copies, waits for them, and re-layouts  3.08 us

profile of v1, /device:TPU:26, one launch (start us, length us, event | category | flops | bytes accessed | tf_op | source)
XLA Modules:
  0.0 94.0 jit_solution(1141266612779961965)
XLA Ops:
  0.0 90.9 %shard_map.64 = bf16[1024,1024]{1,0:T(8,128)(2,1)} custom-call(bf16[1024,4096]{1,0:T(8,128)(2,1)} %tok_hbm.1, bf16[4096,1024]{1,0:T(8,128)(2,1)} %wq_hbm.1, bf16[4096,1024]{1,0:T(8,128)(2,1)} %wk_hbm.1, bf16[4096,1024]{1,0:T(8,128)(2,1)} %wv_hbm.1, f32[1,1024]{1,0:T(1,128)} %bitcast.1, bf16[1024,4096]{1,0:T(8,128)(2,1)} %wo_hbm.1), custom_call_target="tpu_custom_call" | custom-call | tf_op jit(solution)/shard_map/pallas_call | solution.py:266
  90.9 3.1 %copy.8 = bf16[1024,1024]{1,0:T(8,128)(2,1)} copy(bf16[1024,1024]{1,0:T(8,128)(2,1)} %shard_map.64) | data formatting | bytes 4194304

commit v2 on v0

v2 whole, which is shorter than its diff:
```python
import functools

import jax
import jax.numpy as jnp
from jax import lax
from jax.experimental import pallas as pl
from jax.experimental.pallas import tpu as pltpu
from jax.sharding import PartitionSpec as P

HEAD_DIM = 128
CHUNK = 256
PAIR = 2 * HEAD_DIM
ROWS = 512
MESH = pl.DeviceIdType.MESH
BF16 = jnp.bfloat16
F32 = jnp.float32


def kernel(
    n_seq, n_head, nx,
    tok_hbm, wq_hbm, wk_hbm, wv_hbm, gain_ref, wo_hbm, out_hbm,
    tok, kbuf, vbuf, qbuf, q, k, v, att, wcol, acc, pre, total, carried, group,
    x_out, x_in, z_out, z_in, obuf,
    tok_sem, k_sem, v_sem, q_sem, own_sem, o_sem,
    x_ss, x_rs, z_ss, z_rs, ws_ss, ws_rs, wx_ss, wx_rs, wf_ss, wf_rs,
    as_ss, as_rs, ay_ss, ay_rs, af_ss, af_rs,
):
    count, depth = tok.shape
    width = q.shape[1]
    heads = width // HEAD_DIM
    pairs = width // PAIR
    cols = acc.shape[1]
    nt = count // CHUNK
    nu = count // ROWS
    ny = n_head // 2
    nz = n_seq // nx
    share = width // 4
    s = lax.axis_index("seq")
    h = lax.axis_index("head")
    y, c = h // 2, h % 2
    z, x = s // nx, s % nx
    sib = y * 2 + 1 - c
    g = (z % 2) * 2 + x % 2
    flip_x = 1 - 2 * (x % 2)
    flip_z = nx * (1 - 2 * (z % 2))
    quad = [s + flip_x, s + flip_z, s + flip_x + flip_z]

    def remote(src, dst, ss, rs, dev):
        return pltpu.make_async_remote_copy(
            src_ref=src, dst_ref=dst, send_sem=ss, recv_sem=rs,
            device_id=dev, device_id_type=MESH,
        )

    def tok_copy(t):
        rows = pl.ds(pl.multiple_of(t * CHUNK, CHUNK), CHUNK)
        return pltpu.make_async_copy(tok_hbm.at[rows], tok.at[rows], tok_sem.at[t])

    def panel(src, dst, sem, p):
        return pltpu.make_async_copy(
            src.at[:, pl.ds(p * PAIR, PAIR)], dst.at[p % 2], sem.at[p % 2]
        )

    panel(wk_hbm, kbuf, k_sem, 0).start()
    for t in range(nt):
        tok_copy(t).start()
    panel(wv_hbm, vbuf, v_sem, 0).start()

    barrier = pltpu.get_barrier_semaphore()

    def greet(*dev):
        pl.semaphore_signal(barrier, inc=1, device_id=dev, device_id_type=MESH)

    for j in range(1, n_head):
        greet(s, lax.rem(h + j, n_head))
    for j in range(1, nx):
        greet(z * nx + lax.rem(x + j, nx), h)

    @pl.when(z > 0)
    def _():
        greet(s - nx, h)

    @pl.when(z < nz - 1)
    def _():
        greet(s + nx, h)

    greet(quad[2], h)
    pl.semaphore_wait(
        barrier,
        n_head + nx - 1 + (z > 0).astype(jnp.int32) + (z < nz - 1).astype(jnp.int32),
    )

    def block(head):
        return pl.ds(pl.multiple_of(head * cols, cols), cols)

    def rows_of(part):
        return pl.ds(pl.multiple_of(part * share, share), share)

    own_copy = pltpu.make_async_copy(wo_hbm.at[:, block(h)], wcol.at[h], own_sem)

    def ws_copy():
        return remote(wo_hbm.at[:, block(sib)], wcol.at[h], ws_ss, ws_rs, (s, sib))

    def ws_wait():
        remote(wo_hbm.at[:, block(h)], wcol.at[sib], ws_ss, ws_rs, (s, sib)).wait_recv()

    def wx_copy(j, e):
        dest = lax.rem(y + j, ny) * 2 + e
        return remote(
            wo_hbm.at[rows_of(g), block(dest)], wcol.at[h, rows_of(g)],
            wx_ss.at[j - 1, e], wx_rs.at[j - 1, c], (s, dest),
        )

    def source(j, e):
        return lax.rem(y - j + ny, ny) * 2 + e

    def wx_wait(j, e):
        hs = source(j, e)
        remote(
            wo_hbm.at[rows_of(g), block(h)], wcol.at[hs, rows_of(g)],
            wx_ss.at[j - 1, e], wx_rs.at[j - 1, e], (s, hs),
        ).wait_recv()

    def wf_copy(j, e, f):
        part = wcol.at[source(j, e), rows_of(g)]
        return remote(part, part, wf_ss.at[j - 1, e, f], wf_rs.at[j - 1, e, f], (quad[f], h))

    def wf_wait(j, e, f):
        gx, gz = g % 2, g // 2
        other = [gz * 2 + 1 - gx, (1 - gz) * 2 + gx, 3 - g][f]
        part = wcol.at[source(j, e), rows_of(other)]
        remote(
            part, part, wf_ss.at[j - 1, e, f], wf_rs.at[j - 1, e, f], (quad[f], h)
        ).wait_recv()

    for e in range(2):
        for j in range(1, ny):
            wx_copy(j, e).start()

    def x_copy(p, j):
        return remote(
            x_out.at[p], x_in.at[p, j - 1], x_ss.at[p, j - 1], x_rs.at[p, j - 1],
            (z * nx + lax.rem(x + j, nx), h),
        )

    def z_copy(p):
        return remote(
            z_out.at[p], z_in.at[p], z_ss.at[p], z_rs.at[p], (lax.rem(s + nx, n_seq), h)
        )

    stage = [0] * pairs

    def scan_one(p):
        n = stage[p]
        two = slice(2 * p, 2 * p + 2)
        if n == 0:
            x_out[p] = total[two].astype(BF16)
            for j in range(1, nx):
                x_copy(p, j).start()
        elif n == 1:
            whole = total[two]
            before = jnp.zeros_like(whole)
            for j in range(1, nx):
                x_copy(p, j).wait_recv()
                other = x_in[p, j - 1].astype(F32)
                whole = whole + other
                before = before + jnp.where(lax.rem(x - j + nx, nx) < x, other, 0.0)
            carried[two] = before
            group[two] = whole

            @pl.when(z == 0)
            def _():
                z_out[p] = whole.astype(BF16)
                z_copy(p).start()
        elif n <= nz:
            @pl.when(z == n - 1)
            def _():
                z_copy(p).wait_recv()
                got = z_in[p].astype(F32)
                carried[two] += got
                if n < nz:
                    z_out[p] = (got + group[two]).astype(BF16)
                    z_copy(p).start()
        else:
            return
        stage[p] = n + 1

    def scan_step(done):
        for p in range(done):
            scan_one(p)

    def project(w, dst, p, wait):
        @pl.loop(0, nu)
        def _(i):
            if wait:
                for j in range(ROWS // CHUNK):
                    tok_copy(i * (ROWS // CHUNK) + j).wait()
            rows = pl.ds(pl.multiple_of(i * ROWS, ROWS), ROWS)
            dst[rows, p * PAIR:(p + 1) * PAIR] = jnp.dot(
                tok[rows, :], w[...], preferred_element_type=F32
            ).astype(BF16)

    def piece(p, u):
        return pl.ds(u * ROWS, ROWS), pl.ds(p * PAIR, PAIR)

    def as_copy(p, u, head):
        r, l = piece(p, u)
        ref = att.at[head, r, l]
        return remote(ref, ref, as_ss.at[p, u], as_rs.at[p, u], (s, sib))

    def ay_copy(p, u, j, head):
        r, l = piece(p, u)
        ref = att.at[head, r, l]
        return remote(
            ref, ref, ay_ss.at[p, u, j - 1], ay_rs.at[p, u, j - 1],
            (s, lax.rem(y + j, ny) * 2 + c),
        )

    def af_copy(p, u, j, head):
        r, l = piece(p, u)
        ref = att.at[head, r, l]
        return remote(
            ref, ref, af_ss.at[p, u, j - 1], af_rs.at[p, u, j - 1], (s, sib)
        )

    def attention(p):
        keep = lax.broadcasted_iota(jnp.int32, (CHUNK, CHUNK), 0) >= lax.broadcasted_iota(
            jnp.int32, (CHUNK, CHUNK), 1
        )
        for u in range(nu):
            @pl.loop(u * (ROWS // CHUNK), (u + 1) * (ROWS // CHUNK))
            def _(t):
                rows = pl.ds(pl.multiple_of(t * CHUNK, CHUNK), CHUNK)
                for hd in (2 * p, 2 * p + 1):
                    lanes = slice(hd * HEAD_DIM, (hd + 1) * HEAD_DIM)
                    qh, kh, vh = q[rows, lanes], k[rows, lanes], v[rows, lanes]
                    scores = lax.dot_general(
                        qh, kh, (((1,), (1,)), ((), ())), preferred_element_type=F32
                    )
                    scores = jnp.where(keep, scores, 0.0).astype(BF16)
                    prior = (carried[hd] + pre[t, hd]).astype(BF16)
                    raw = jnp.dot(scores, vh, preferred_element_type=F32) + jnp.dot(
                        qh, prior, preferred_element_type=F32
                    )
                    power = jnp.mean(raw * raw, axis=-1, keepdims=True)
                    att[h, rows, lanes] = (
                        raw * lax.rsqrt(power + 1e-6) * gain_ref[:, lanes]
                    ).astype(BF16)

            for j in range(1, ny):
                ay_copy(p, u, j, h).start()
            as_copy(p, u, h).start()

    def forward(p):
        for u in range(nu):
            for j in range(1, ny):
                head = source(j, c)
                ay_copy(p, u, j, head).wait_recv()
                af_copy(p, u, j, head).start()

    for p in range(pairs):
        panel(wk_hbm, kbuf, k_sem, p).wait()
        if p == 0:
            panel(wq_hbm, qbuf, q_sem, 0).start()
        if p + 1 < pairs:
            panel(wk_hbm, kbuf, k_sem, p + 1).start()
        project(kbuf.at[p % 2], k, p, p == 0)
        scan_step(p)
        panel(wv_hbm, vbuf, v_sem, p).wait()
        if p + 1 < pairs:
            panel(wv_hbm, vbuf, v_sem, p + 1).start()
        project(vbuf.at[p % 2], v, p, False)
        for hd in (2 * p, 2 * p + 1):
            lanes = slice(hd * HEAD_DIM, (hd + 1) * HEAD_DIM)
            run = jnp.zeros((HEAD_DIM, HEAD_DIM), F32)
            for t in range(nt):
                pre[t, hd] = run
                run = run + lax.dot_general(
                    k[t * CHUNK:(t + 1) * CHUNK, lanes], v[t * CHUNK:(t + 1) * CHUNK, lanes],
                    (((0,), (0,)), ((), ())), preferred_element_type=F32,
                )
            total[hd] = run
        scan_step(p + 1)
        panel(wq_hbm, qbuf, q_sem, p).wait()
        if p + 1 < pairs:
            panel(wq_hbm, qbuf, q_sem, p + 1).start()
        if p == 0:
            own_copy.start()
            ws_copy().start()
        project(qbuf.at[p % 2], q, p, False)
        scan_step(p + 1)
        if p > 0:
            while stage[p - 1] <= nz:
                scan_one(p - 1)
            attention(p - 1)
        if p == 1:
            for e in range(2):
                for j in range(1, ny):
                    wx_wait(j, e)
                    for f in range(3):
                        wf_copy(j, e, f).start()

    last = pairs - 1
    scan_step(pairs)
    own_copy.wait()
    ws_wait()

    def add(t, head, lanes, first):
        rows = pl.ds(pl.multiple_of(t * CHUNK, CHUNK), CHUNK)
        term = jnp.dot(att[head, rows, lanes], wcol[head, lanes, :], preferred_element_type=F32)
        acc[rows, :] = term if first else acc[rows, :] + term

    ready = last * PAIR

    def add_all(head, lanes, first):
        @pl.loop(0, nt)
        def _(t):
            add(t, head, lanes, first)

    add_all(h, slice(0, ready), True)
    scan_step(pairs)
    if pairs > 1:
        forward(0)
    for p in range(last):
        for u in range(nu):
            as_copy(p, u, sib).wait_recv()
    while stage[last] <= nz:
        scan_one(last)
    attention(last)
    add_all(sib, slice(0, ready), False)
    for p in range(1, last):
        if p == 1:
            forward(p)
    add_all(h, slice(ready, width), False)
    for u in range(nu):
        as_copy(last, u, sib).wait_recv()
    add_all(sib, slice(ready, width), False)
    for e in range(2):
        for j in range(1, ny):
            for f in range(3):
                wf_wait(j, e, f)

    def out_copy(t):
        rows = pl.ds(t * CHUNK, CHUNK)
        return pltpu.make_async_copy(obuf.at[t], out_hbm.at[rows], o_sem.at[t])

    for p in range(pairs):
        lanes = slice(p * PAIR, (p + 1) * PAIR)
        for u in range(nu):
            if p >= 2 or p == last:
                for j in range(1, ny):
                    head = source(j, c)
                    ay_copy(p, u, j, head).wait_recv()
                    af_copy(p, u, j, head).start()
            for e in range(2):
                for j in range(1, ny):
                    if e == 0:
                        head = source(j, c)
                    else:
                        head = source(j, 1 - c)
                        af_copy(p, u, j, head).wait_recv()

                    @pl.loop(u * (ROWS // CHUNK), (u + 1) * (ROWS // CHUNK))
                    def _(t):
                        add(t, head, lanes, False)

            if p == last:
                for t in range(u * (ROWS // CHUNK), (u + 1) * (ROWS // CHUNK)):
                    obuf[t] = acc[t * CHUNK:(t + 1) * CHUNK, :].astype(BF16)
                    out_copy(t).start()

    for t in range(nt):
        out_copy(t).wait()
    ws_copy().wait_send()
    for e in range(2):
        for j in range(1, ny):
            wx_copy(j, e).wait_send()
            for f in range(3):
                wf_copy(j, e, f).wait_send()
    for p in range(pairs):
        for j in range(1, nx):
            x_copy(p, j).wait_send()

        @pl.when(z < nz - 1)
        def _():
            z_copy(p).wait_send()

        for u in range(nu):
            as_copy(p, u, h).wait_send()
            for j in range(1, ny):
                ay_copy(p, u, j, h).wait_send()
                af_copy(p, u, j, source(j, c)).wait_send()


def local(n_seq, n_head, nx, tokens, w_query, w_key, w_value, norm_gain, w_out):
    count, depth = tokens.shape
    width = w_query.shape[1]
    heads, pairs = width // HEAD_DIM, width // PAIR
    cols = w_out.shape[1] // n_head
    nt, nu, ny = count // CHUNK, count // ROWS, n_head // 2
    dma = pltpu.SemaphoreType.DMA
    hbm = pl.BlockSpec(memory_space=pl.ANY)
    vmem = pl.BlockSpec(memory_space=pltpu.VMEM)
    state = (HEAD_DIM, HEAD_DIM)
    return pl.pallas_call(
        functools.partial(kernel, n_seq, n_head, nx),
        out_shape=jax.ShapeDtypeStruct((count, cols), BF16),
        in_specs=[hbm, hbm, hbm, hbm, vmem, hbm],
        out_specs=hbm,
        scratch_shapes=[
            pltpu.VMEM((count, depth), BF16),
            pltpu.VMEM((2, depth, PAIR), BF16),
            pltpu.VMEM((2, depth, PAIR), BF16),
            pltpu.VMEM((2, depth, PAIR), BF16),
            pltpu.VMEM((count, width), BF16),
            pltpu.VMEM((count, width), BF16),
            pltpu.VMEM((count, width), BF16),
            pltpu.VMEM((n_head, count, width), BF16),
            pltpu.VMEM((n_head, width, cols), BF16),
            pltpu.VMEM((count, cols), F32),
            pltpu.VMEM((nt, heads, *state), F32),
            pltpu.VMEM((heads, *state), F32),
            pltpu.VMEM((heads, *state), F32),
            pltpu.VMEM((heads, *state), F32),
            pltpu.VMEM((pairs, 2, *state), BF16),
            pltpu.VMEM((pairs, nx - 1, 2, *state), BF16),
            pltpu.VMEM((pairs, 2, *state), BF16),
            pltpu.VMEM((pairs, 2, *state), BF16),
            pltpu.VMEM((nt, CHUNK, cols), BF16),
            dma((nt,)), dma((2,)), dma((2,)), dma((2,)), dma, dma((nt,)),
            dma((pairs, nx - 1)), dma((pairs, nx - 1)), dma((pairs,)), dma((pairs,)),
            dma, dma, dma((ny - 1, 2)), dma((ny - 1, 2)),
            dma((ny - 1, 2, 3)), dma((ny - 1, 2, 3)),
            dma((pairs, nu)), dma((pairs, nu)),
            dma((pairs, nu, ny - 1)), dma((pairs, nu, ny - 1)),
            dma((pairs, nu, ny - 1)), dma((pairs, nu, ny - 1)),
        ],
        compiler_params=pltpu.CompilerParams(
            collective_id=0, has_side_effects=True, vmem_limit_bytes=63 * 2**20
        ),
    )(tokens, w_query, w_key, w_value, norm_gain.reshape(1, width), w_out)


def solution(mesh):
    n_seq, n_head = mesh.shape["seq"], mesh.shape["head"]
    nx = 1 << ((n_seq.bit_length() - 1) // 2)
    in_specs = (
        P("seq", None), P(None, "head"), P(None, "head"), P(None, "head"),
        P("head"), P("head", None),
    )
    return jax.shard_map(
        functools.partial(local, n_seq, n_head, nx), mesh=mesh, in_specs=in_specs,
        out_specs=P("seq", "head"), check_vma=False,
    )
```

time: 212 us -> 115 us (0.54)
  Pallas kernels: 0 us -> 111 us
  waiting for transfers between devices: 95.6 us -> 0 us
  matrix products: 68.5 us -> 0 us
  other arithmetic: 14.6 us -> 0 us
  local copies, waits for them, and re-layouts: 17.5 us -> 3.08 us
  between operations: 13.5 us -> 0.01 us
    pallas_call x0 -> x1, Pallas kernels: none -> 111 us  [local(): pl.pallas_call(functools.partial(kernel, n_seq, n_head, nx), out_shape=ja...]
    reduce_scatter x1 -> x0, waiting for transfers between devices: 72.8 us -> none  [local(): lax.psum_scatter(lax.dot_general(w_out, attended, (((0,), (1,)), ((), ())...]
    dot_general x7 -> x0, matrix products: 68.5 us -> none  [the longest x1 14.7 us: local(): lax.dot_general(w_out, attended, (((0,), (1,)), ((), ())), preferred_elem...]
    all_gather x1 -> x0, waiting for transfers between devices: 22.7 us -> none  [prefix(): everything = lax.all_gather(shard.astype(jnp.bfloat16), axis)]
    select_n x8 -> x0, other arithmetic: 9.87 us -> none  [hop(): return jnp.where(reached, new, before)]
    slice x2 -> x0, local copies, waits for them, and re-layouts: 5.03 us -> none  [the longest x1 4.29 us: local(): running[:-1]]
    another operation x1 -> x0, other arithmetic: 3.89 us -> none  [local(): running = jnp.cumsum(states, axis=0)]
    unnamed x11 -> x1, local copies, waits for them, and re-layouts: 6.44 us -> 3.08 us
  transfers between devices with their start and end apart: 2 -> 0, of which waited for: 2 -> 0; matrix products, arithmetic and copies ran while one was open for 12% -> 0% of each run, Pallas kernels for 0% -> 0%
where the time goes in v2:
time: 115 us; the launch traced here: 114 us
  Pallas kernels  111 us (97%)
  local copies, waits for them, and re-layouts  3.08 us (3%)
    pallas_call x1, Pallas kernels, local(): pl.pallas_call(functools.partial(kernel, n_seq, n_head, nx), out_shape=ja...  111 us
    unnamed x1, local copies, waits for them, and re-layouts  3.08 us

profile of v2, /device:TPU:26, one launch (start us, length us, event | category | flops | bytes accessed | tf_op | source)
XLA Modules:
  0.0 113.9 jit_solution(9153371722258477283)
XLA Ops:
  0.0 110.8 %shard_map.64 = bf16[1024,1024]{1,0:T(8,128)(2,1)} custom-call(bf16[1024,4096]{1,0:T(8,128)(2,1)} %tok_hbm.1, bf16[4096,1024]{1,0:T(8,128)(2,1)} %wq_hbm.1, bf16[4096,1024]{1,0:T(8,128)(2,1)} %wk_hbm.1, bf16[4096,1024]{1,0:T(8,128)(2,1)} %wv_hbm.1, f32[1,1024]{1,0:T(1,128)} %bitcast.1, bf16[1024,4096]{1,0:T(8,128)(2,1)} %wo_hbm.1), custom_call_target="tpu_custom_call" | custom-call | tf_op jit(solution)/shard_map/pallas_call | solution.py:404
  110.8 3.1 %copy.8 = bf16[1024,1024]{1,0:T(8,128)(2,1)} copy(bf16[1024,1024]{1,0:T(8,128)(2,1)} %shard_map.64) | data formatting | bytes 4194304

commit v3 on v1

--- a/solution.py
+++ b/solution.py
@@ -18,12 +18,12 @@
 
 
 def kernel(
-    n_seq, n_head,
+    n_seq, n_head, nx,
     tok_hbm, wq_hbm, wk_hbm, wv_hbm, gain_ref, wo_hbm, out_hbm,
     tok, kbuf, vbuf, wq, wo, q, k, v, att, pre, total, carried,
-    scan_out, scan_in, sib_out, sib_in, y_out, y_in, own, obuf,
+    group, x_out, x_in, z_out, z_in, sib_out, sib_in, y_out, y_in, own, obuf,
     tok_sem, k_sem, v_sem, wq_sem, wo_sem, o_sem,
-    scan_ss, scan_rs, sib_ss, sib_rs, y_ss, y_rs,
+    x_ss, x_rs, z_ss, z_rs, sib_ss, sib_rs, y_ss, y_rs,
 ):
     count, depth = tok.shape
     width = q.shape[1]
@@ -32,11 +32,18 @@
     cols = wo.shape[1] // n_head
     nt = count // CHUNK
     ny = n_head // 2
-    rounds = (n_seq - 1).bit_length()
+    nz = n_seq // nx
     s = lax.axis_index("seq")
     h = lax.axis_index("head")
     y, c = h // 2, h % 2
     sib = y * 2 + 1 - c
+    z, x = s // nx, s % nx
+
+    def remote(src, dst, ss, rs, dev):
+        return pltpu.make_async_remote_copy(
+            src_ref=src, dst_ref=dst, send_sem=ss, recv_sem=rs,
+            device_id=dev, device_id_type=MESH,
+        )
 
     def tok_copy(t):
         rows = pl.ds(pl.multiple_of(t * CHUNK, CHUNK), CHUNK)
@@ -61,53 +68,73 @@
     for j in range(1, ny):
         peer = lax.rem(y + j, ny) * 2 + c
         pl.semaphore_signal(barrier, inc=1, device_id=(s, peer), device_id_type=MESH)
-    for r in range(rounds):
-        d = 1 << r
-
-        @pl.when(s + d < n_seq)
-        def _():
-            pl.semaphore_signal(barrier, inc=1, device_id=(s + d, h), device_id_type=MESH)
-
-        @pl.when(s >= d)
-        def _():
-            pl.semaphore_signal(barrier, inc=1, device_id=(s - d, h), device_id_type=MESH)
-
-        expected += (s + d < n_seq).astype(jnp.int32) + (s >= d).astype(jnp.int32)
+    for j in range(1, nx):
+        pl.semaphore_signal(
+            barrier, inc=1, device_id=(z * nx + lax.rem(x + j, nx), h), device_id_type=MESH
+        )
+
+    @pl.when(z > 0)
+    def _():
+        pl.semaphore_signal(barrier, inc=1, device_id=(s - nx, h), device_id_type=MESH)
+
+    @pl.when(z < nz - 1)
+    def _():
+        pl.semaphore_signal(barrier, inc=1, device_id=(s + nx, h), device_id_type=MESH)
+
+    expected += nx - 1 + (z > 0).astype(jnp.int32) + (z < nz - 1).astype(jnp.int32)
     pl.semaphore_wait(barrier, expected)
 
-    def scan_copy(p, r):
-        return pltpu.make_async_remote_copy(
-            src_ref=scan_out.at[p, r], dst_ref=scan_in.at[p, r],
-            send_sem=scan_ss.at[p, r], recv_sem=scan_rs.at[p, r],
-            device_id=(lax.rem(s + (1 << r), n_seq), h), device_id_type=MESH,
-        )
-
-    def scan_send(p, r):
-        @pl.when(s + (1 << r) < n_seq)
-        def _():
-            scan_out[p, r] = (carried[2 * p:2 * p + 2] + total[2 * p:2 * p + 2]).astype(BF16)
-            scan_copy(p, r).start()
-
-    def scan_recv(p, r):
-        @pl.when(s >= (1 << r))
-        def _():
-            scan_copy(p, r).wait_recv()
-            carried[2 * p:2 * p + 2] += scan_in[p, r].astype(F32)
+    def x_copy(p, j):
+        return remote(
+            x_out.at[p], x_in.at[p, j - 1], x_ss.at[p, j - 1], x_rs.at[p, j - 1],
+            (z * nx + lax.rem(x + j, nx), h),
+        )
+
+    def z_copy(p):
+        return remote(
+            z_out.at[p], z_in.at[p], z_ss.at[p], z_rs.at[p], (lax.rem(s + nx, n_seq), h)
+        )
 
     stage = [0] * pairs
+
+    def scan_one(p):
+        n = stage[p]
+        two = slice(2 * p, 2 * p + 2)
+        if n == 0:
+            x_out[p] = total[two].astype(BF16)
+            for j in range(1, nx):
+                x_copy(p, j).start()
+        elif n == 1:
+            whole = total[two]
+            before = jnp.zeros_like(whole)
+            for j in range(1, nx):
+                x_copy(p, j).wait_recv()
+                other = x_in[p, j - 1].astype(F32)
+                whole = whole + other
+                before = before + jnp.where(lax.rem(x - j + nx, nx) < x, other, 0.0)
+            carried[two] = before
+            group[two] = whole
+
+            @pl.when(z == 0)
+            def _():
+                z_out[p] = whole.astype(BF16)
+                z_copy(p).start()
+        elif n <= nz:
+            @pl.when(z == n - 1)
+            def _():
+                z_copy(p).wait_recv()
+                got = z_in[p].astype(F32)
+                carried[two] += got
+                if n < nz:
+                    z_out[p] = (got + group[two]).astype(BF16)
+                    z_copy(p).start()
+        else:
+            return
+        stage[p] = n + 1
 
     def scan_step(done):
         for p in range(done):
-            r = stage[p]
-            if r > rounds:
-                continue
-            if r > 0:
-                scan_recv(p, r - 1)
-            if r < rounds:
-                scan_send(p, r)
-            stage[p] = r + 1
-
-    carried[...] = jnp.zeros_like(carried)
+            scan_one(p)
 
     def project(w, dst, p, wait):
         @pl.loop(0, count // ROWS)
@@ -125,8 +152,9 @@
         if p + 1 < pairs:
             panel(wk_hbm, kbuf, k_sem, p + 1).start()
             panel(wv_hbm, vbuf, v_sem, p + 1).start()
-        if p == min(1, pairs - 1):
+        if p == pairs - 2:
             wq_copy.start()
+        if p == pairs - 1:
             wo_copy.start()
         project(kbuf.at[p % 2], k, p, p == 0)
         if p > 0:
@@ -160,7 +188,7 @@
     for t in range(AHEAD):
         project_q(t)
         scan_step(pairs)
-    while min(stage) <= rounds:
+    while min(stage) <= nz:
         scan_step(pairs)
     wo_copy.wait()
 
@@ -246,25 +274,26 @@
         for j in range(1, ny):
             y_copy(t, j).wait_send()
     for p in range(pairs):
-        for r in range(rounds):
-            @pl.when(s + (1 << r) < n_seq)
-            def _():
-                scan_copy(p, r).wait_send()
-
-
-def local(n_seq, n_head, tokens, w_query, w_key, w_value, norm_gain, w_out):
+        for j in range(1, nx):
+            x_copy(p, j).wait_send()
+
+        @pl.when(z < nz - 1)
+        def _():
+            z_copy(p).wait_send()
+
+
+def local(n_seq, n_head, nx, tokens, w_query, w_key, w_value, norm_gain, w_out):
     count, depth = tokens.shape
     width = w_query.shape[1]
     heads, pairs = width // HEAD_DIM, width // PAIR
     features = w_out.shape[1]
     cols = features // n_head
     nt, ny = count // CHUNK, n_head // 2
-    rounds = (n_seq - 1).bit_length()
     dma = pltpu.SemaphoreType.DMA
     hbm = pl.BlockSpec(memory_space=pl.ANY)
     vmem = pl.BlockSpec(memory_space=pltpu.VMEM)
     return pl.pallas_call(
-        functools.partial(kernel, n_seq, n_head),
+        functools.partial(kernel, n_seq, n_head, nx),
         out_shape=jax.ShapeDtypeStruct((count, cols), BF16),
         in_specs=[hbm, hbm, hbm, hbm, vmem, hbm],
         out_specs=hbm,
@@ -281,8 +310,11 @@
             pltpu.VMEM((nt, heads, HEAD_DIM, HEAD_DIM), F32),
             pltpu.VMEM((heads, HEAD_DIM, HEAD_DIM), F32),
             pltpu.VMEM((heads, HEAD_DIM, HEAD_DIM), F32),
-            pltpu.VMEM((pairs, rounds, 2, HEAD_DIM, HEAD_DIM), BF16),
-            pltpu.VMEM((pairs, rounds, 2, HEAD_DIM, HEAD_DIM), BF16),
+            pltpu.VMEM((heads, HEAD_DIM, HEAD_DIM), F32),
+            pltpu.VMEM((pairs, 2, HEAD_DIM, HEAD_DIM), BF16),
+            pltpu.VMEM((pairs, nx - 1, 2, HEAD_DIM, HEAD_DIM), BF16),
+            pltpu.VMEM((pairs, 2, HEAD_DIM, HEAD_DIM), BF16),
+            pltpu.VMEM((pairs, 2, HEAD_DIM, HEAD_DIM), BF16),
             pltpu.VMEM((2, ny, CHUNK, cols), BF16),
             pltpu.VMEM((nt, ny, CHUNK, cols), BF16),
             pltpu.VMEM((nt, ny - 1, CHUNK, cols), BF16),
@@ -290,7 +322,7 @@
             pltpu.VMEM((count, cols), F32),
             pltpu.VMEM((2, CHUNK, cols), BF16),
             dma((nt,)), dma((2,)), dma((2,)), dma, dma, dma((2,)),
-            dma((pairs, rounds)), dma((pairs, rounds)),
+            dma((pairs, nx - 1)), dma((pairs, nx - 1)), dma((pairs,)), dma((pairs,)),
             dma((nt, ny)), dma((nt, ny)),
             dma((nt, ny - 1)), dma((nt, ny - 1)),
         ],
@@ -302,11 +334,12 @@
 
 def solution(mesh):
     n_seq, n_head = mesh.shape["seq"], mesh.shape["head"]
+    nx = 1 << ((n_seq.bit_length() - 1) // 2)
     in_specs = (
         P("seq", None), P(None, "head"), P(None, "head"), P(None, "head"),
         P("head"), P("head", None),
     )
     return jax.shard_map(
-        functools.partial(local, n_seq, n_head), mesh=mesh, in_specs=in_specs,
+        functools.partial(local, n_seq, n_head, nx), mesh=mesh, in_specs=in_specs,
         out_specs=P("seq", "head"), check_vma=False,
     )

time: 94.2 us -> 96.7 us (1.027)
  Pallas kernels: 90.9 us -> 93.2 us
    pallas_call x1, Pallas kernels: 90.9 us -> 93.2 us  [local(): pl.pallas_call(functools.partial(kernel, n_seq, n_head, nx), out_shape=ja...]
where the time goes in v3:
time: 96.7 us; the launch traced here: 96.3 us
  Pallas kernels  93.2 us (96%)
  local copies, waits for them, and re-layouts  3.08 us (3%)
    pallas_call x1, Pallas kernels, local(): pl.pallas_call(functools.partial(kernel, n_seq, n_head, nx), out_shape=ja...  93.2 us
    unnamed x1, local copies, waits for them, and re-layouts  3.08 us

profile of v3, /device:TPU:26, one launch (start us, length us, event | category | flops | bytes accessed | tf_op | source)
XLA Modules:
  0.0 96.3 jit_solution(8848240597617600214)
XLA Ops:
  0.0 93.2 %shard_map.64 = bf16[1024,1024]{1,0:T(8,128)(2,1)} custom-call(bf16[1024,4096]{1,0:T(8,128)(2,1)} %tok_hbm.1, bf16[4096,1024]{1,0:T(8,128)(2,1)} %wq_hbm.1, bf16[4096,1024]{1,0:T(8,128)(2,1)} %wk_hbm.1, bf16[4096,1024]{1,0:T(8,128)(2,1)} %wv_hbm.1, f32[1,1024]{1,0:T(1,128)} %bitcast.1, bf16[1024,4096]{1,0:T(8,128)(2,1)} %wo_hbm.1), custom_call_target="tpu_custom_call" | custom-call | tf_op jit(solution)/shard_map/pallas_call | solution.py:295
  93.2 3.1 %copy.8 = bf16[1024,1024]{1,0:T(8,128)(2,1)} copy(bf16[1024,1024]{1,0:T(8,128)(2,1)} %shard_map.64) | data formatting | bytes 4194304
